TPU v7x, 32 devices: a whole 2x2x4 slice. The times are simulated.
32 devices in a mesh: prow: 8 (over z, x), pcol: 4 (over y, core).
Axes of the slice: x: 2, y: 2, z: 4, core: 2. Of those that a mesh axis runs over, the one named last changes fastest.
Arguments:
- sigma_top: bfloat16 [8192, 8192], P('prow', 'pcol'), may hold values from -400 to 400, as said below
- panel_par: bfloat16 [8192, 1024], P('prow', 'pcol'), may hold values from -0.119628906 to 0.119628906
- panel_kid: bfloat16 [8192, 2048], P('prow', 'pcol'), may hold values from -0.119628906 to 0.119628906
- link_kid: bfloat16 [8, 256, 256], P('pcol'), may hold values from -0.23925781 to 0.23925781
- dinv_par: float32 [4, 256, 256], P('pcol'), may hold values from -6 to 6
- dinv_kid: float32 [8, 256, 256], P('pcol'), may hold values from -6 to 6
- mask_par: int32 [4, 32], P('pcol', 'prow'), may hold values 0 or 1
- mask_kid: int32 [8, 32], P('pcol', 'prow'), may hold values 0 or 1
Outputs:
- sigma_par: bfloat16 [8192, 1024], P('prow', 'pcol')
- diag_par: float32 [4, 256, 256], P('pcol')
- sigma_kid: bfloat16 [8192, 2048], P('prow', 'pcol')
- link_sigma: float32 [8, 256, 256], P('pcol')
- diag_kid: float32 [8, 256, 256], P('pcol')
Inputs may be any that keep to these rules, and one draw needn't show every extreme that they name: `sigma_top`: symmetric.
All inputs are finite; a program needn't handle non-finite values. No bound on the sum of `mask_par` or of `mask_kid` on one device may be relied on, other than what follows from the above.
Results may differ from a plain program's by a relative error of at most 0.015.
Values may be sent and summed in bfloat16 or wider, within the bound.
A program may use at most 64 MiB of HBM per device.

v0:
```python
import jax
import jax.numpy as jnp
from jax import lax
from jax.sharding import PartitionSpec as P

KIDS = 2


def expand_rows(mask, width):
    count, blocks = mask.shape
    spread = jnp.broadcast_to(
        mask.T.astype(jnp.float32)[:, None, :, None], (blocks, width, count, width)
    )
    return spread.reshape(blocks * width, count * width)


def batch_mult(left, right):
    return jnp.einsum("cab,cbd->cad", left, right, precision=lax.Precision.HIGHEST)


def batch_tmult(left, right):
    return jnp.einsum("cba,cbd->cad", left, right, precision=lax.Precision.HIGHEST)


def on_device(sigma_top, panel_par, panel_kid, link_kid, dinv_par, dinv_kid, mask_par, mask_kid):
    width = dinv_par.shape[1]
    par_here = dinv_par.shape[0]
    kid_here = dinv_kid.shape[0]
    row_count = sigma_top.shape[0]
    kid_pattern = mask_kid * jnp.repeat(mask_par, KIDS, axis=0)
    par_rows = expand_rows(mask_par, width)
    kid_rows = expand_rows(kid_pattern, width)
    low_par = panel_par * par_rows.astype(jnp.bfloat16)
    low_kid = panel_kid * kid_rows.astype(jnp.bfloat16)
    sigma_rows = lax.all_gather(sigma_top, "pcol", axis=1, tiled=True)
    prod_par = jnp.dot(
        sigma_rows,
        lax.all_gather(low_par, "prow", axis=0, tiled=True),
        preferred_element_type=jnp.float32,
    )
    prod_kid = jnp.dot(
        sigma_rows,
        lax.all_gather(low_kid, "prow", axis=0, tiled=True),
        preferred_element_type=jnp.float32,
    )
    sigma_par = (-prod_par * par_rows).astype(jnp.bfloat16)
    par_blocks = sigma_par.reshape(row_count, par_here, width)
    par_spread = jnp.repeat(par_blocks, KIDS, axis=1)
    carried = jnp.einsum("rcb,cbd->rcd", par_spread, link_kid, preferred_element_type=jnp.float32)
    sigma_kid = (-(prod_kid + carried.reshape(row_count, kid_here * width)) * kid_rows).astype(
        jnp.bfloat16
    )
    low_par3 = low_par.reshape(row_count, par_here, width)
    low_kid3 = low_kid.reshape(row_count, kid_here, width)
    kid_blocks = sigma_kid.reshape(row_count, kid_here, width)
    part_par = jnp.einsum("rpb,rpd->pbd", low_par3, par_blocks, preferred_element_type=jnp.float32)
    part_cross = jnp.einsum(
        "rcb,rcd->cbd", par_spread, low_kid3, preferred_element_type=jnp.float32
    )
    part_kid = jnp.einsum("rcb,rcd->cbd", low_kid3, kid_blocks, preferred_element_type=jnp.float32)
    link_wide = link_kid.astype(jnp.float32)
    sum_par = lax.psum(part_par.astype(jnp.bfloat16), "prow").astype(jnp.float32)
    diag_par = dinv_par - sum_par
    diag_spread = jnp.repeat(diag_par, KIDS, axis=0)
    cross_sum, kid_sum = (
        lax.psum(part_cross.astype(jnp.bfloat16), "prow").astype(jnp.float32),
        lax.psum(part_kid.astype(jnp.bfloat16), "prow").astype(jnp.float32),
    )
    link_sigma = -(cross_sum + batch_mult(diag_spread, link_wide))
    diag_kid = dinv_kid - kid_sum - batch_tmult(link_wide, link_sigma)
    return (sigma_par, diag_par, sigma_kid, link_sigma, diag_kid)


def solution(mesh):
    placed = (
        P("prow", "pcol"),
        P("prow", "pcol"),
        P("prow", "pcol"),
        P("pcol", None, None),
        P("pcol", None, None),
        P("pcol", None, None),
        P("pcol", "prow"),
        P("pcol", "prow"),
    )
    return jax.shard_map(
        on_device,
        mesh=mesh,
        in_specs=placed,
        out_specs=(
            P("prow", "pcol"),
            P("pcol", None, None),
            P("prow", "pcol"),
            P("pcol", None, None),
            P("pcol", None, None),
        ),
        check_vma=False,
    )
```

profile of v0, /device:TPU:20, one launch (start us, length us, event | category | flops | bytes accessed | tf_op | source)
XLA Modules:
  0.0 419.3 jit_solution(7698292222596817835)
XLA Ops:
  7.3 0.7 bitcast_convert_fusion
  8.1 2.0 broadcast_multiply_fusion
  10.2 0.7 all-gather.6.cloned.1.call-update
  11.0 1.3 copy.13
  12.3 0.3 broadcast_in_dim.25
  12.6 0.5 copy.29
  13.1 0.4 copy-done.3
  13.5 1.2 convert_multiply_fusion
  14.8 69.6 %all-gather.4.cloned.1.call-done = bf16[8192,256]{1,0:T(8,128)(2,1)} async-done(((bf16[1024,256]{1,0:T(8,128)(2,1)}), bf16[8192,256]{1,0:T(8,128)(2,1)}) %all-gather.4.cloned.1.call-update) | async-done | bytes 4194320 | tf_op jit(solution)/shard_map/all_gather | solution.py:38
  84.4 105.7 %all-gather.6.cloned.1.call-done = bf16[1024,8192]{1,0:T(8,128)(2,1)} async-done(((bf16[1024,2048]{1,0:T(8,128)(2,1)}), bf16[1024,8192]{1,0:T(8,128)(2,1)}) %all-gather.6.cloned.1.call-update) | async-done | bytes 16777232 | tf_op jit(solution)/shard_map/all_gather | solution.py:35
  190.1 11.6 %fusion.4 = bf16[256,1024]{1,0:T(8,128)(2,1)S(1)} fusion(bf16[8192,256]{1,0:T(8,128)(2,1)} %all-gather.4.cloned.1.call-done, bf16[1024,8192]{1,0:T(8,128)(2,1)} %all-gather.6.cloned.1.call-done, f32[1024]{0:T(1024)S(1)} %bitcast.58), kind=kOutput, calls=%fused_computation.6 | convolution fusion | flops 4295753728 | bytes 21499904 | tf_op jit(solution)/shard_map/dot_general | solution.py:36
  201.7 1.0 fusion.7
  202.7 2.5 convolution_convert_fusion.1
  205.2 1.9 fusion.9
  207.0 110.8 %all-gather.8.cloned.1.call-done = bf16[8192,512]{0,1:T(8,128)(2,1)} async-done(((bf16[1024,512]{0,1:T(8,128)(2,1)}), bf16[8192,512]{0,1:T(8,128)(2,1)}) %all-gather.8.cloned.1.call-update) | async-done | bytes 8388624 | tf_op jit(solution)/shard_map/all_gather | solution.py:43
  317.8 15.2 %fusion.2 = bf16[1024,512]{0,1:T(8,128)(2,1)S(1)} fusion(f32[1024,512]{0,1:T(8,128)S(1)} %bitcast.48, f32[2,1024,256]{1,2,0:T(8,128)} %fusion.9, bf16[8192,512]{0,1:T(8,128)(2,1)} %all-gather.8.cloned.1.call-done, bf16[1024,8192]{1,0:T(8,128)(2,1)} %all-gather.6.cloned.1.call-done), kind=kOutput, calls=%fused_computation.3 | convolution fusion | flops 8592031744 | bytes 30408704 | tf_op jit(solution)/shard_map/dot_general | solution.py:41
  333.1 1.0 copy-done.7
  334.1 1.2 convolution_convert_fusion
  335.3 1.0 copy.20
  336.3 2.3 copy.21
  338.5 69.4 %all-reduce.3.cloned.1.call-done = (bf16[1,256,256]{2,1,0:T(8,128)(2,1)}, bf16[2,256,256]{2,1,0:T(8,128)(2,1)}, bf16[2,256,256]{2,1,0:T(8,128)(2,1)}) async-done(((bf16[1,256,256]{2,1,0:T(8,128)(2,1)}, bf16[2,256,256]{2,1,0:T(8,128)(2,1)}, bf16[2,256,256]{2,1,0:T(8,128)(2,1)}), (bf16[1,256,256]{2,1,0:T(8,128)(2,1)}, bf16[2,256,256]{2,1,0:T(8,128)(2,1)}, ...) | async-done | bytes 655376 | tf_op jit(solution)/shard_map/psum | solution.py:62
  408.0 0.9 convert_subtract_fusion
  408.9 1.5 fusion.6
  410.4 2.4 fusion.5
  (33 shorter events, 0.4 us)
Async XLA Ops:
  7.2 198.0 %copy-start = (bf16[2,256,256]{2,1,0:T(8,128)(2,1)S(1)}, bf16[2,256,256]{2,1,0:T(8,128)(2,1)}, u32[]{:S(2)}) copy-start(bf16[2,256,256]{2,1,0:T(8,128)(2,1)} %param.11) | copy-start | bytes 786436
  7.2 5.1 %copy-start.11 = (s32[1,4]{1,0:T(1,128)S(1)}, s32[1,4]{1,0:T(1,128)}, u32[]{:S(2)}) copy-start(s32[1,4]{1,0:T(1,128)} %param.14) | copy-start | bytes 52
  7.2 3.8 copy-start.6
  7.2 5.1 %copy-start.10 = (s32[2,4]{1,0:T(2,128)S(1)}, s32[2,4]{1,0:T(2,128)}, u32[]{:S(2)}) copy-start(s32[2,4]{1,0:T(2,128)} %param.15) | copy-start | bytes 100
  7.2 77.2 %all-gather.4.cloned.1.call-start = ((), (), s32[]{:S(2)}) async-start(), calls=%async_computation | async-start | bytes 4718592 | tf_op jit(solution)/shard_map/all_gather | solution.py:38
  10.2 179.9 %all-gather.6.cloned.1.call-start = ((), (), s32[]{:S(2)}) async-start(), calls=%async_computation.1 | async-start | bytes 20971520 | tf_op jit(solution)/shard_map/all_gather | solution.py:35
  10.9 306.9 %all-gather.8.cloned.1.call-start = ((), (), s32[]{:S(2)}) async-start(), calls=%async_computation.2 | async-start | bytes 9437184 | tf_op jit(solution)/shard_map/all_gather | solution.py:43
  12.3 1.2 copy-start.3
  14.7 186.9 %copy-start.1 = (bf16[1024,256]{1,0:T(8,128)(2,1)S(1)}, bf16[1024,256]{1,0:T(8,128)(2,1)}, u32[]{:S(2)}) copy-start(bf16[1024,256]{1,0:T(8,128)(2,1)} %broadcast_multiply_fusion) | copy-start | bytes 1572868
  14.8 393.2 %all-reduce.3.cloned.1.call-start = ((), (), s32[]{:S(2)}) async-start(), calls=%async_computation.3 | async-start | bytes 1310720 | tf_op jit(solution)/shard_map/psum | solution.py:62
  317.8 16.3 %copy-start.2 = (bf16[1024,512]{0,1:T(8,128)(2,1)S(1)}, bf16[1024,512]{0,1:T(8,128)(2,1)}, u32[]{:S(2)}) copy-start(bf16[1024,512]{0,1:T(8,128)(2,1)} %convert_multiply_fusion) | copy-start | bytes 3145732
  333.1 1.0 copy-start.7
  333.1 74.9 %copy-start.9 = (f32[1,256,256]{2,1,0:T(8,128)S(1)}, f32[1,256,256]{2,1,0:T(8,128)}, u32[]{:S(2)}) copy-start(f32[1,256,256]{2,1,0:T(8,128)} %param.12) | copy-start | bytes 786436
  333.1 77.3 %copy-start.8 = (f32[2,256,256]{2,1,0:T(8,128)S(1)}, f32[2,256,256]{2,1,0:T(8,128)}, u32[]{:S(2)}) copy-start(f32[2,256,256]{2,1,0:T(8,128)} %param.13) | copy-start | bytes 1572868
  408.9 3.9 copy-start.5
  410.4 2.4 copy-start.4
Sparse Core Ops, SparseCore 0:
  10.7 73.5 all-gather.3
  85.9 104.0 all-gather.5
  192.8 124.9 all-gather.7
  335.4 72.5 all-reduce.2
where the time goes:
time: 422 us; the launch traced here: 419 us
  waiting for transfers between devices  356 us (84%)
  matrix products  37.2 us (9%)
  between operations  13.9 us (3%)
  local copies, waits for them, and re-layouts  6.89 us (2%)
  other arithmetic  4.93 us (1%)
    all_gather x1, waiting for transfers between devices, on_device(): lax.all_gather(low_kid, 'prow', axis=0, tiled=True)  111 us
    all_gather x1, waiting for transfers between devices, on_device(): sigma_rows = lax.all_gather(sigma_top, 'pcol', axis=1, tiled=True)  106 us
    all_gather x1, waiting for transfers between devices, on_device(): lax.all_gather(low_par, 'prow', axis=0, tiled=True)  69.6 us
    psum x1, waiting for transfers between devices, on_device(): lax.psum(part_par.astype(jnp.bfloat16), 'prow').astype(jnp.float32)  69.4 us
    dot_general x1, matrix products, on_device(): jnp.dot(sigma_rows, lax.all_gather(low_kid, 'prow', axis=0, tiled=True),...  15.2 us
    dot_general x1, matrix products, on_device(): jnp.dot(sigma_rows, lax.all_gather(low_par, 'prow', axis=0, tiled=True),...  11.6 us
  transfers between devices with their start and end apart: 4, of which 4 were waited for; matrix products, arithmetic and copies ran while one was open for 6% of the time, Pallas kernels for 0%

commit v1 on v0

--- a/solution.py
+++ b/solution.py
@@ -1,9 +1,223 @@
+import functools
+
 import jax
 import jax.numpy as jnp
 from jax import lax
+from jax.experimental import pallas as pl
+from jax.experimental.pallas import tpu as pltpu
 from jax.sharding import PartitionSpec as P
 
 KIDS = 2
+PIECES = 4
+MESH = pl.DeviceIdType.MESH
+
+
+def gather_kernel(line, chips, tile_ref, low_ref, sig_ref, all_ref, s_self, y_send, y_recv, c_send,
+                  c_recv, z_send, z_recv, x_send, x_recv):
+    row = lax.axis_index("prow")
+    col = lax.axis_index("pcol")
+    place, side = row // 2, row % 2
+    chip, core = col // 2, col % 2
+    height, width = tile_ref.shape
+    depth = low_ref.shape[0]
+    after, before = (place + 1) % line, (place + line - 1) % line
+    dev_x = (place * 2 + 1 - side, col)
+    dev_up = (after * 2 + side, col)
+    dev_down = (before * 2 + side, col)
+    dev_core = (row, chip * 2 + 1 - core)
+    dev_y = [(row, (chip + d) % chips * 2 + core) for d in range(1, chips)]
+
+    barrier = pltpu.get_barrier_semaphore()
+    for dev in [dev_x, dev_up, dev_down, dev_core] + dev_y:
+        pl.semaphore_signal(barrier, inc=1, device_id=dev, device_id_type=MESH)
+    pl.semaphore_wait(barrier, 4 + len(dev_y))
+
+    hs = height // PIECES
+    ds = depth // PIECES
+
+    def sig_at(owner, s):
+        start = pl.multiple_of(owner * width, width)
+        return sig_ref.at[pl.ds(s * hs, hs), pl.ds(start, width)]
+
+    def low_at(block, s):
+        start = pl.multiple_of(block * depth + s * ds, ds)
+        return all_ref.at[pl.ds(start, ds), :]
+
+    def remote(src, dst, send, recv, dev):
+        return pltpu.make_async_remote_copy(src_ref=src, dst_ref=dst, send_sem=send,
+                                            recv_sem=recv, device_id=dev, device_id_type=MESH)
+
+    def tile_piece(s):
+        return tile_ref.at[pl.ds(s * hs, hs), :]
+
+    def low_piece(s):
+        return low_ref.at[pl.ds(s * ds, ds), :]
+
+    def to_x(slot, block, s, src):
+        return remote(src, low_at(block, s), x_send.at[slot, s], x_recv.at[slot, s], dev_x)
+
+    def to_z(way, t, block, s, src):
+        return remote(src, low_at(block, s), z_send.at[way, t, s], z_recv.at[way, t, s],
+                      dev_up if way == 0 else dev_down)
+
+    def to_y(d, s):
+        return remote(tile_piece(s), sig_at(col, s), y_send.at[d - 1, s], y_recv.at[d - 1, s],
+                      dev_y[d - 1])
+
+    def to_core(d, s, owner, src):
+        return remote(src, sig_at(owner, s), c_send.at[d, s], c_recv.at[d, s], dev_core)
+
+    can_up = place < line - 1
+    can_down = place > 0
+    for s in range(PIECES):
+        pl.when(can_up)(lambda: to_z(0, 0, row, s, low_piece(s)).start())
+        pl.when(can_down)(lambda: to_z(1, 0, row, s, low_piece(s)).start())
+        to_x(0, row, s, low_piece(s)).start()
+        for d in range(1, chips):
+            to_y(d, s).start()
+        to_core(0, s, col, tile_piece(s)).start()
+    own_sig = pltpu.make_async_copy(
+        tile_ref, sig_ref.at[:, pl.ds(pl.multiple_of(col * width, width), width)], s_self.at[0])
+    own_low = pltpu.make_async_copy(
+        low_ref, all_ref.at[pl.ds(pl.multiple_of(row * depth, depth), depth), :], s_self.at[1])
+    own_sig.start()
+    own_low.start()
+
+    def from_line(way, t):
+        block = row - 2 * t if way == 0 else row + 2 * t
+        here = place - t >= 0 if way == 0 else place + t < line
+        onward = (here & can_up) if way == 0 else (here & can_down)
+        slot = t if way == 0 else line - 1 + t
+        return block, here, onward, slot
+
+    def pass_low(way, t, s):
+        block, here, onward, slot = from_line(way, t)
+
+        @pl.when(here)
+        def _():
+            to_z(way, t - 1, block, s, low_at(block, s)).wait_recv()
+            to_x(slot, block, s, low_at(block, s)).start()
+        if t < line - 1:
+            @pl.when(onward)
+            def _():
+                to_z(way, t, block, s, low_at(block, s)).start()
+
+    def pass_sig(d, s):
+        owner = (chip + chips - d) % chips * 2 + core
+        to_y(d, s).wait_recv()
+        to_core(d, s, owner, sig_at(owner, s)).start()
+
+    lows = [(t, s) for t in range(1, line) for s in range(PIECES)]
+    sigs = [(d, s) for s in range(PIECES) for d in range(1, chips)]
+    done = 0
+    for i, (t, s) in enumerate(lows):
+        pass_low(0, t, s)
+        pass_low(1, t, s)
+        upto = (i + 1) * len(sigs) // len(lows)
+        for d, p in sigs[done:upto]:
+            pass_sig(d, p)
+        done = upto
+
+    for s in range(PIECES):
+        to_x(0, row, s, low_piece(s)).wait()
+        for d in range(chips):
+            to_core(d, s, col, tile_piece(s)).wait()
+        for d in range(1, chips):
+            to_y(d, s).wait_send()
+        pl.when(can_up)(lambda: to_z(0, 0, row, s, low_piece(s)).wait_send())
+        pl.when(can_down)(lambda: to_z(1, 0, row, s, low_piece(s)).wait_send())
+        for t in range(1, line):
+            for way in range(2):
+                block, here, onward, slot = from_line(way, t)
+
+                @pl.when(here)
+                def _():
+                    to_x(slot, block, s, low_at(block, s)).wait()
+                if t < line - 1:
+                    @pl.when(onward)
+                    def _():
+                        to_z(way, t, block, s, low_at(block, s)).wait_send()
+    own_sig.wait()
+    own_low.wait()
+
+
+def gather_all(rows, cols, tile, low):
+    line, chips = rows // 2, cols // 2
+    height, width = tile.shape
+    depth, count = low.shape
+    dma = pltpu.SemaphoreType.DMA
+    return pl.pallas_call(
+        functools.partial(gather_kernel, line, chips),
+        out_shape=(
+            jax.ShapeDtypeStruct((height, cols * width), tile.dtype),
+            jax.ShapeDtypeStruct((rows * depth, count), low.dtype),
+        ),
+        in_specs=[pl.BlockSpec(memory_space=pl.ANY)] * 2,
+        out_specs=[pl.BlockSpec(memory_space=pl.ANY)] * 2,
+        scratch_shapes=[
+            dma((2,)),
+            dma((max(chips - 1, 1), PIECES)), dma((max(chips - 1, 1), PIECES)),
+            dma((chips, PIECES)), dma((chips, PIECES)),
+            dma((2, line, PIECES)), dma((2, line, PIECES)),
+            dma((2 * line - 1, PIECES)), dma((2 * line - 1, PIECES)),
+        ],
+        compiler_params=pltpu.CompilerParams(collective_id=0, has_side_effects=True),
+    )(tile, low)
+
+
+def sum_kernel(count, part_ref, out_ref, got, s_send, s_recv, g_send, g_recv):
+    row = lax.axis_index("prow")
+    col = lax.axis_index("pcol")
+    size = part_ref.shape[0] // count
+    peers = [((row + d) % count, col) for d in range(1, count)]
+    barrier = pltpu.get_barrier_semaphore()
+    for dev in peers:
+        pl.semaphore_signal(barrier, inc=1, device_id=dev, device_id_type=MESH)
+    pl.semaphore_wait(barrier, len(peers))
+
+    def share(block):
+        return pl.ds(pl.multiple_of(block * size, size), size)
+
+    def scatter(d):
+        return pltpu.make_async_remote_copy(
+            src_ref=part_ref.at[share((row + d) % count), :], dst_ref=got.at[d - 1],
+            send_sem=s_send.at[d - 1], recv_sem=s_recv.at[d - 1], device_id=peers[d - 1],
+            device_id_type=MESH)
+
+    def spread(d):
+        return pltpu.make_async_remote_copy(
+            src_ref=out_ref.at[share(row), :], dst_ref=out_ref.at[share(row), :],
+            send_sem=g_send.at[d - 1], recv_sem=g_recv.at[d - 1], device_id=peers[d - 1],
+            device_id_type=MESH)
+
+    for d in range(1, count):
+        scatter(d).start()
+    total = part_ref[share(row), :].astype(jnp.float32)
+    for d in range(1, count):
+        scatter(d).wait_recv()
+        total = total + got[d - 1].astype(jnp.float32)
+    out_ref[share(row), :] = total.astype(out_ref.dtype)
+    for d in range(1, count):
+        spread(d).start()
+    for d in range(1, count):
+        scatter(d).wait_send()
+        spread(d).wait()
+
+
+def sum_parts(count, parts):
+    size = parts.shape[0] // count
+    dma = pltpu.SemaphoreType.DMA
+    return pl.pallas_call(
+        functools.partial(sum_kernel, count),
+        out_shape=jax.ShapeDtypeStruct(parts.shape, parts.dtype),
+        in_specs=[pl.BlockSpec(memory_space=pltpu.VMEM)],
+        out_specs=pl.BlockSpec(memory_space=pltpu.VMEM),
+        scratch_shapes=[
+            pltpu.VMEM((count - 1, size, parts.shape[1]), parts.dtype),
+            dma((count - 1,)), dma((count - 1,)), dma((count - 1,)), dma((count - 1,)),
+        ],
+        compiler_params=pltpu.CompilerParams(collective_id=1, has_side_effects=True),
+    )(parts)
 
 
 def expand_rows(mask, width):
@@ -22,7 +236,7 @@
     return jnp.einsum("cba,cbd->cad", left, right, precision=lax.Precision.HIGHEST)
 
 
-def on_device(sigma_top, panel_par, panel_kid, link_kid, dinv_par, dinv_kid, mask_par, mask_kid):
+def on_device(rows, cols, sigma_top, panel_par, panel_kid, link_kid, dinv_par, dinv_kid, mask_par, mask_kid):
     width = dinv_par.shape[1]
     par_here = dinv_par.shape[0]
     kid_here = dinv_kid.shape[0]
@@ -32,17 +246,11 @@
     kid_rows = expand_rows(kid_pattern, width)
     low_par = panel_par * par_rows.astype(jnp.bfloat16)
     low_kid = panel_kid * kid_rows.astype(jnp.bfloat16)
-    sigma_rows = lax.all_gather(sigma_top, "pcol", axis=1, tiled=True)
-    prod_par = jnp.dot(
-        sigma_rows,
-        lax.all_gather(low_par, "prow", axis=0, tiled=True),
-        preferred_element_type=jnp.float32,
-    )
-    prod_kid = jnp.dot(
-        sigma_rows,
-        lax.all_gather(low_kid, "prow", axis=0, tiled=True),
-        preferred_element_type=jnp.float32,
-    )
+    low_all = jnp.concatenate([low_par, low_kid], axis=1)
+    sigma_rows, low_rows = gather_all(rows, cols, sigma_top, low_all)
+    prod = jnp.dot(sigma_rows, low_rows, preferred_element_type=jnp.float32)
+    prod_par = prod[:, : par_here * width]
+    prod_kid = prod[:, par_here * width :]
     sigma_par = (-prod_par * par_rows).astype(jnp.bfloat16)
     par_blocks = sigma_par.reshape(row_count, par_here, width)
     par_spread = jnp.repeat(par_blocks, KIDS, axis=1)
@@ -59,13 +267,14 @@
     )
     part_kid = jnp.einsum("rcb,rcd->cbd", low_kid3, kid_blocks, preferred_element_type=jnp.float32)
     link_wide = link_kid.astype(jnp.float32)
-    sum_par = lax.psum(part_par.astype(jnp.bfloat16), "prow").astype(jnp.float32)
+    parts = jnp.concatenate([part_par, part_cross, part_kid], axis=0).astype(jnp.bfloat16)
+    total = sum_parts(rows, parts.reshape(-1, width)).astype(jnp.float32)
+    total = total.reshape(parts.shape)
+    sum_par = total[:par_here]
+    cross_sum = total[par_here : par_here + kid_here]
+    kid_sum = total[par_here + kid_here :]
     diag_par = dinv_par - sum_par
     diag_spread = jnp.repeat(diag_par, KIDS, axis=0)
-    cross_sum, kid_sum = (
-        lax.psum(part_cross.astype(jnp.bfloat16), "prow").astype(jnp.float32),
-        lax.psum(part_kid.astype(jnp.bfloat16), "prow").astype(jnp.float32),
-    )
     link_sigma = -(cross_sum + batch_mult(diag_spread, link_wide))
     diag_kid = dinv_kid - kid_sum - batch_tmult(link_wide, link_sigma)
     return (sigma_par, diag_par, sigma_kid, link_sigma, diag_kid)
@@ -83,7 +292,7 @@
         P("pcol", "prow"),
     )
     return jax.shard_map(
-        on_device,
+        functools.partial(on_device, mesh.shape["prow"], mesh.shape["pcol"]),
         mesh=mesh,
         in_specs=placed,
         out_specs=(

time: 422 us -> 272 us (0.64)
  waiting for transfers between devices: 356 us -> 0 us
  Pallas kernels: 0 us -> 215 us
  between operations: 13.9 us -> 0.89 us
  local copies, waits for them, and re-layouts: 6.89 us -> 17.8 us
  matrix products: 37.2 us -> 26.9 us
  other arithmetic: 4.93 us -> 10.8 us
    all_gather x3 -> x0, waiting for transfers between devices: 286 us -> none  [the longest x1 111 us: on_device(): lax.all_gather(low_kid, 'prow', axis=0, tiled=True)]
    pallas_call x0 -> x2, Pallas kernels: none -> 215 us  [the longest x1 179 us: gather_all(): pl.pallas_call(functools.partial(gather_kernel, line, chips), out_shape=(...]
    psum x1 -> x0, waiting for transfers between devices: 69.4 us -> none  [on_device(): lax.psum(part_par.astype(jnp.bfloat16), 'prow').astype(jnp.float32)]
    convert_element_type x0 -> x3, other arithmetic: none -> 7.38 us  [the longest x1 4 us: on_device(): (-(prod_kid + carried.reshape(row_count, kid_here * width)) * kid_rows).a...]
    dot_general x2 -> x1, matrix products: 26.8 us -> 20.3 us  [on_device(): prod = jnp.dot(sigma_rows, low_rows, preferred_element_type=jnp.float32)]
    unnamed x30 -> x37, local copies, waits for them, and re-layouts: 6.55 us -> 9.44 us
  transfers between devices with their start and end apart: 4 -> 0, of which waited for: 4 -> 0; matrix products, arithmetic and copies ran while one was open for 6% -> 0% of each run, Pallas kernels for 0% -> 0%
where the time goes in v1:
time: 272 us
  Pallas kernels  215 us (79%)
  matrix products  26.9 us (10%)
  local copies, waits for them, and re-layouts  17.8 us (7%)
  other arithmetic  10.8 us (4%)
    pallas_call x1, Pallas kernels, gather_all(): pl.pallas_call(functools.partial(gather_kernel, line, chips), out_shape=(...  179 us
    pallas_call x1, Pallas kernels, sum_parts(): pl.pallas_call(functools.partial(sum_kernel, count), out_shape=jax.ShapeD...  36.5 us
    dot_general x1, matrix products, on_device(): prod = jnp.dot(sigma_rows, low_rows, preferred_element_type=jnp.float32)  20.3 us
    unnamed x37, local copies, waits for them, and re-layouts  9.44 us

profile of v1, /device:TPU:20, one launch (start us, length us, event | category | flops | bytes accessed | tf_op | source)
XLA Modules:
  0.0 271.5 jit_solution(3557988871832619954)
XLA Ops:
  0.6 0.7 convert_bitcast_fusion
  1.5 0.6 broadcast_in_dim.24
  2.3 1.0 copy-done.10
  3.6 0.4 copy-done.14
  4.6 0.8 copy-done.3
  5.4 1.3 pad_maximum_fusion.low_ref
  6.7 178.7 %shard_map.119 = (bf16[1024,8192]{1,0:T(8,128)(2,1)}, bf16[8192,768]{1,0:T(8,128)(2,1)}) custom-call(bf16[1024,2048]{1,0:T(8,128)(2,1)} %tile_ref.1, bf16[1024,768]{1,0:T(8,128)(2,1)} %pad_maximum_fusion.low_ref), custom_call_target="tpu_custom_call" | custom-call | tf_op jit(solution)/shard_map/pallas_call | solution.py:149
  185.4 20.3 %fusion.13 = f32[1024,768]{0,1:T(8,128)} fusion(bf16[1024,8192]{1,0:T(8,128)(2,1)} %get-tuple-element.7, bf16[8192,768]{1,0:T(8,128)(2,1)} %get-tuple-element.8), kind=kOutput, calls=%fused_computation.28 | convolution fusion | flops 12884901888 | bytes 32505856 | tf_op jit(solution)/shard_map/dot_general | solution.py:251
  205.7 2.1 fusion.6
  207.8 2.0 copy.25
  209.8 2.9 %fusion.7 = f32[2,1024,256]{1,2,0:T(8,128)} fusion(bf16[2,256,256]{2,1,0:T(8,128)(2,1)S(1)} %copy-done, bf16[1024,256]{1,0:T(8,128)(2,1)} %copy.25), kind=kOutput, calls=%fused_computation.17 | convolution fusion | flops 268435456 | bytes 2883584 | tf_op jit(solution)/shard_map/rcb,cbd->rcd/dot_general | solution.py:257
  212.7 2.9 %copy.30 = f32[1024,512]{1,0:T(8,128)} copy(f32[1024,512]{0,1:T(8,128)} %bitcast.45) | data formatting | bytes 4194304 | tf_op jit(solution)/shard_map/reshape | solution.py:258
  215.6 3.2 %slice.33 = f32[1024,512]{0,1:T(8,128)} slice(f32[1024,768]{0,1:T(8,128)} %fusion.13), slice={[0:1024], [256:768]} | slice | bytes 4194304 | tf_op jit(solution)/shard_map/slice | solution.py:253
  218.8 2.9 %copy.31 = f32[1024,512]{1,0:T(8,128)} copy(f32[1024,512]{0,1:T(8,128)} %slice.33) | data formatting | bytes 4194304
  221.7 4.0 %multiply_convert_fusion = bf16[1024,512]{1,0:T(8,128)(2,1)} fusion(f32[1024,512]{1,0:T(8,128)S(1)} %bitcast.43, f32[1024,512]{1,0:T(8,128)} %copy.31, f32[1024,512]{1,0:T(8,128)} %copy.30), kind=kLoop, calls=%fused_computation | loop fusion | flops 2097152 | bytes 7340032 | tf_op jit(solution)/shard_map/convert_element_type | solution.py:258
  225.7 1.3 copy.32
  227.0 1.8 convolution_convert_fusion
  228.8 0.5 convolution_convert_fusion.1
  229.8 0.9 pad_maximum_fusion.1
  230.7 36.5 %shard_map.120 = bf16[1280,256]{1,0:T(8,128)(2,1)} custom-call(bf16[1280,256]{1,0:T(8,128)(2,1)} %bitcast.46), custom_call_target="tpu_custom_call" | custom-call | tf_op jit(solution)/shard_map/pallas_call | solution.py:210
  267.2 1.2 convert_element_type.45
  269.3 0.4 copy-done.12
  269.9 0.6 fusion
  270.5 1.0 copy.26
  (40 shorter events, 2.4 us)
Async XLA Ops:
  0.6 209.2 %copy-start = (bf16[2,256,256]{2,1,0:T(8,128)(2,1)S(1)}, bf16[2,256,256]{2,1,0:T(8,128)(2,1)}, u32[]{:S(2)}) copy-start(bf16[2,256,256]{2,1,0:T(8,128)(2,1)} %param.11) | copy-start | bytes 786436
  2.1 1.2 copy-start.10
  3.3 0.7 copy-start.14
  3.3 1.1 copy-start.11
  4.6 0.8 copy-start.3
  225.7 1.3 copy-start.7
  225.7 3.1 %copy-start.6 = (bf16[1024,256]{1,0:T(8,128)(2,1)S(1)}, bf16[1024,256]{1,0:T(8,128)(2,1)}, u32[]{:S(2)}) copy-start(bf16[1024,256]{1,0:T(8,128)(2,1)} %copy.25) | copy-start | bytes 1572868
  227.0 1.8 copy-start.8
  227.0 2.4 copy-start.2
  227.0 2.4 copy-start.4
  229.8 38.7 %copy-start.13 = (f32[1,256,256]{2,1,0:T(8,128)S(1)}, f32[1,256,256]{2,1,0:T(8,128)}, u32[]{:S(2)}) copy-start(f32[1,256,256]{2,1,0:T(8,128)} %param.12) | copy-start | bytes 786436
  267.2 1.3 copy-start.1
  268.5 0.7 copy-start.9
  268.5 1.1 copy-start.12
  269.0 1.5 copy-start.5

commit v2 on v1

--- a/solution.py
+++ b/solution.py
@@ -8,12 +8,12 @@
 from jax.sharding import PartitionSpec as P
 
 KIDS = 2
-PIECES = 4
+PIECES = 8
 MESH = pl.DeviceIdType.MESH
 
 
 def gather_kernel(line, chips, tile_ref, low_ref, sig_ref, all_ref, s_self, y_send, y_recv, c_send,
-                  c_recv, z_send, z_recv, x_send, x_recv):
+                  c_recv, z_send, z_recv, w_send, w_recv, x_send, x_recv):
     row = lax.axis_index("prow")
     col = lax.axis_index("pcol")
     place, side = row // 2, row % 2
@@ -60,6 +60,11 @@
         return remote(src, low_at(block, s), z_send.at[way, t, s], z_recv.at[way, t, s],
                       dev_up if way == 0 else dev_down)
 
+    def to_w(way, t, block):
+        piece = low_at(block, 0)
+        return remote(piece, piece, w_send.at[way, t], w_recv.at[way, t],
+                      dev_up if way == 0 else dev_down)
+
     def to_y(d, s):
         return remote(tile_piece(s), sig_at(col, s), y_send.at[d - 1, s], y_recv.at[d - 1, s],
                       dev_y[d - 1])
@@ -69,10 +74,11 @@
 
     can_up = place < line - 1
     can_down = place > 0
+    other = row + 1 - 2 * side
     for s in range(PIECES):
+        to_x(0, row, s, low_piece(s)).start()
         pl.when(can_up)(lambda: to_z(0, 0, row, s, low_piece(s)).start())
         pl.when(can_down)(lambda: to_z(1, 0, row, s, low_piece(s)).start())
-        to_x(0, row, s, low_piece(s)).start()
         for d in range(1, chips):
             to_y(d, s).start()
         to_core(0, s, col, tile_piece(s)).start()
@@ -96,11 +102,22 @@
         @pl.when(here)
         def _():
             to_z(way, t - 1, block, s, low_at(block, s)).wait_recv()
-            to_x(slot, block, s, low_at(block, s)).start()
+            if s > 0:
+                to_x(slot, block, s, low_at(block, s)).start()
         if t < line - 1:
             @pl.when(onward)
             def _():
                 to_z(way, t, block, s, low_at(block, s)).start()
+        if s == 1:
+            beside = block + other - row
+
+            @pl.when(here)
+            def _():
+                to_w(way, t - 1, beside).wait_recv()
+            if t < line - 1:
+                @pl.when(onward)
+                def _():
+                    to_w(way, t, beside).start()
 
     def pass_sig(d, s):
         owner = (chip + chips - d) % chips * 2 + core
@@ -109,6 +126,9 @@
 
     lows = [(t, s) for t in range(1, line) for s in range(PIECES)]
     sigs = [(d, s) for s in range(PIECES) for d in range(1, chips)]
+    to_x(0, row, 0, low_piece(0)).wait_recv()
+    pl.when(can_up)(lambda: to_w(0, 0, other).start())
+    pl.when(can_down)(lambda: to_w(1, 0, other).start())
     done = 0
     for i, (t, s) in enumerate(lows):
         pass_low(0, t, s)
@@ -119,7 +139,12 @@
         done = upto
 
     for s in range(PIECES):
-        to_x(0, row, s, low_piece(s)).wait()
+        if s > 0:
+            to_x(0, row, s, low_piece(s)).wait()
+        else:
+            to_x(0, row, s, low_piece(s)).wait_send()
+            pl.when(can_up)(lambda: to_w(0, 0, other).wait_send())
+            pl.when(can_down)(lambda: to_w(1, 0, other).wait_send())
         for d in range(chips):
             to_core(d, s, col, tile_piece(s)).wait()
         for d in range(1, chips):
@@ -130,13 +155,16 @@
             for way in range(2):
                 block, here, onward, slot = from_line(way, t)
 
-                @pl.when(here)
-                def _():
-                    to_x(slot, block, s, low_at(block, s)).wait()
+                if s > 0:
+                    @pl.when(here)
+                    def _():
+                        to_x(slot, block, s, low_at(block, s)).wait()
                 if t < line - 1:
                     @pl.when(onward)
                     def _():
                         to_z(way, t, block, s, low_at(block, s)).wait_send()
+                        if s == 0:
+                            to_w(way, t, block + other - row).wait_send()
     own_sig.wait()
     own_low.wait()
 
@@ -159,10 +187,83 @@
             dma((max(chips - 1, 1), PIECES)), dma((max(chips - 1, 1), PIECES)),
             dma((chips, PIECES)), dma((chips, PIECES)),
             dma((2, line, PIECES)), dma((2, line, PIECES)),
+            dma((2, line)), dma((2, line)),
             dma((2 * line - 1, PIECES)), dma((2 * line - 1, PIECES)),
         ],
         compiler_params=pltpu.CompilerParams(collective_id=0, has_side_effects=True),
     )(tile, low)
+
+
+def sweep_kernel(par_here, sig_ref, low_ref, own_ref, keep_ref, link_ref, par_ref, kid_ref,
+                 part_ref, acc):
+    step = pl.program_id(0)
+    width = link_ref.shape[1]
+    kid_here = link_ref.shape[0]
+    prod = jnp.dot(sig_ref[...], low_ref[...], preferred_element_type=jnp.float32)
+
+    @pl.when(step == 0)
+    def _():
+        acc[...] = jnp.zeros_like(acc)
+
+    def span(block):
+        return slice(block * width, (block + 1) * width)
+
+    def rows_dot(left, right):
+        return lax.dot_general(left, right, (((0,), (0,)), ((), ())),
+                               preferred_element_type=jnp.float32)
+
+    for p in range(par_here):
+        keep = keep_ref[:, span(p)].astype(jnp.float32)
+        sig_par = (-prod[:, span(p)] * keep).astype(jnp.bfloat16)
+        par_ref[:, span(p)] = sig_par
+        acc[p] += rows_dot(own_ref[:, span(p)], sig_par)
+        for c in range(p * KIDS, (p + 1) * KIDS):
+            at = span(par_here + c)
+            low = own_ref[:, at]
+            carried = jnp.dot(sig_par, link_ref[c], preferred_element_type=jnp.float32)
+            sig_kid = -(prod[:, at] + carried) * keep_ref[:, at].astype(jnp.float32)
+            sig_kid = sig_kid.astype(jnp.bfloat16)
+            kid_ref[:, span(c)] = sig_kid
+            acc[par_here + c] += rows_dot(sig_par, low)
+            acc[par_here + kid_here + c] += rows_dot(low, sig_kid)
+
+    @pl.when(step == pl.num_programs(0) - 1)
+    def _():
+        part_ref[...] = acc[...].astype(part_ref.dtype)
+
+
+def sweep(par_here, sigma_rows, low_rows, own, keep, link):
+    kid_here, width, _ = link.shape
+    height, order = sigma_rows.shape
+    count = own.shape[1]
+    blocks = par_here + 2 * kid_here
+
+    def by_row(columns):
+        return pl.BlockSpec((width, columns), lambda i: (i, 0))
+
+    return pl.pallas_call(
+        functools.partial(sweep_kernel, par_here),
+        grid=(height // width,),
+        out_shape=(
+            jax.ShapeDtypeStruct((height, par_here * width), jnp.bfloat16),
+            jax.ShapeDtypeStruct((height, kid_here * width), jnp.bfloat16),
+            jax.ShapeDtypeStruct((blocks, width, width), jnp.bfloat16),
+        ),
+        in_specs=[
+            by_row(order),
+            pl.BlockSpec((order, count), lambda i: (0, 0)),
+            by_row(count),
+            by_row(count),
+            pl.BlockSpec(link.shape, lambda i: (0, 0, 0)),
+        ],
+        out_specs=[
+            by_row(par_here * width),
+            by_row(kid_here * width),
+            pl.BlockSpec((blocks, width, width), lambda i: (0, 0, 0)),
+        ],
+        scratch_shapes=[pltpu.VMEM((blocks, width, width), jnp.float32)],
+        compiler_params=pltpu.CompilerParams(vmem_limit_bytes=56 * 1024 * 1024),
+    )(sigma_rows, low_rows, own, keep, link)
 
 
 def sum_kernel(count, part_ref, out_ref, got, s_send, s_recv, g_send, g_recv):
@@ -240,34 +341,14 @@
     width = dinv_par.shape[1]
     par_here = dinv_par.shape[0]
     kid_here = dinv_kid.shape[0]
-    row_count = sigma_top.shape[0]
     kid_pattern = mask_kid * jnp.repeat(mask_par, KIDS, axis=0)
-    par_rows = expand_rows(mask_par, width)
-    kid_rows = expand_rows(kid_pattern, width)
-    low_par = panel_par * par_rows.astype(jnp.bfloat16)
-    low_kid = panel_kid * kid_rows.astype(jnp.bfloat16)
-    low_all = jnp.concatenate([low_par, low_kid], axis=1)
-    sigma_rows, low_rows = gather_all(rows, cols, sigma_top, low_all)
-    prod = jnp.dot(sigma_rows, low_rows, preferred_element_type=jnp.float32)
-    prod_par = prod[:, : par_here * width]
-    prod_kid = prod[:, par_here * width :]
-    sigma_par = (-prod_par * par_rows).astype(jnp.bfloat16)
-    par_blocks = sigma_par.reshape(row_count, par_here, width)
-    par_spread = jnp.repeat(par_blocks, KIDS, axis=1)
-    carried = jnp.einsum("rcb,cbd->rcd", par_spread, link_kid, preferred_element_type=jnp.float32)
-    sigma_kid = (-(prod_kid + carried.reshape(row_count, kid_here * width)) * kid_rows).astype(
-        jnp.bfloat16
-    )
-    low_par3 = low_par.reshape(row_count, par_here, width)
-    low_kid3 = low_kid.reshape(row_count, kid_here, width)
-    kid_blocks = sigma_kid.reshape(row_count, kid_here, width)
-    part_par = jnp.einsum("rpb,rpd->pbd", low_par3, par_blocks, preferred_element_type=jnp.float32)
-    part_cross = jnp.einsum(
-        "rcb,rcd->cbd", par_spread, low_kid3, preferred_element_type=jnp.float32
-    )
-    part_kid = jnp.einsum("rcb,rcd->cbd", low_kid3, kid_blocks, preferred_element_type=jnp.float32)
+    keep = jnp.concatenate(
+        [expand_rows(mask_par, width), expand_rows(kid_pattern, width)], axis=1
+    ).astype(jnp.bfloat16)
+    low_own = jnp.concatenate([panel_par, panel_kid], axis=1) * keep
+    sigma_rows, low_rows = gather_all(rows, cols, sigma_top, low_own)
+    sigma_par, sigma_kid, parts = sweep(par_here, sigma_rows, low_rows, low_own, keep, link_kid)
     link_wide = link_kid.astype(jnp.float32)
-    parts = jnp.concatenate([part_par, part_cross, part_kid], axis=0).astype(jnp.bfloat16)
     total = sum_parts(rows, parts.reshape(-1, width)).astype(jnp.float32)
     total = total.reshape(parts.shape)
     sum_par = total[:par_here]

time: 272 us -> 250 us (0.919)
  Pallas kernels: 215 us -> 241 us
  matrix products: 26.9 us -> 1.03 us
  local copies, waits for them, and re-layouts: 17.8 us -> 3.1 us
  other arithmetic: 10.8 us -> 4.2 us
    dot_general x5 -> x0, matrix products: 25.8 us -> none  [the longest x1 20.3 us: on_device(): prod = jnp.dot(sigma_rows, low_rows, preferred_element_type=jnp.float32)]
    pallas_call x0 -> x1, Pallas kernels: none -> 23.9 us  [sweep(): pl.pallas_call(functools.partial(sweep_kernel, par_here), grid=(height //...]
    unnamed x37 -> x23, local copies, waits for them, and re-layouts: 9.44 us -> 1.91 us
    convert_element_type x5 -> x0, other arithmetic: 6.87 us -> none  [the longest x1 4 us: on_device(): (-(prod_kid + carried.reshape(row_count, kid_here * width)) * kid_rows).a...]
    reshape x2 -> x0, local copies, waits for them, and re-layouts: 4.21 us -> none  [the longest x1 2.9 us: on_device(): carried.reshape(row_count, kid_here * width)]
    slice x1 -> x0, local copies, waits for them, and re-layouts: 3.17 us -> none  [on_device(): prod_kid = prod[:, par_here * width:]]
where the time goes in v2:
time: 250 us
  Pallas kernels  241 us (96%)
  other arithmetic  4.2 us (2%)
  local copies, waits for them, and re-layouts  3.1 us (1%)
    pallas_call x1, Pallas kernels, gather_all(): pl.pallas_call(functools.partial(gather_kernel, line, chips), out_shape=(...  180 us
    pallas_call x1, Pallas kernels, sum_parts(): pl.pallas_call(functools.partial(sum_kernel, count), out_shape=jax.ShapeD...  36.5 us
    pallas_call x1, Pallas kernels, sweep(): pl.pallas_call(functools.partial(sweep_kernel, par_here), grid=(height //...  23.9 us

profile of v2, /device:TPU:20, one launch (start us, length us, event | category | flops | bytes accessed | tf_op | source)
XLA Modules:
  0.0 249.9 jit_solution(14959019647316834855)
XLA Ops:
  0.7 0.8 fusion.4
  1.5 0.1 copy.13
  1.6 0.6 broadcast_in_dim.21
  2.2 0.2 copy.20
  2.5 0.1 broadcast_bitcast_fusion
  2.5 0.2 broadcast_in_dim.20
  2.8 2.1 pad_maximum_fusion
  4.9 180.3 %shard_map.119 = (bf16[1024,8192]{1,0:T(8,128)(2,1)}, bf16[8192,768]{1,0:T(8,128)(2,1)}) custom-call(bf16[1024,2048]{1,0:T(8,128)(2,1)} %tile_ref.1, bf16[1024,768]{1,0:T(8,128)(2,1)} %get-tuple-element.21.low_ref.own_ref), custom_call_target="tpu_custom_call" | custom-call | tf_op jit(solution)/shard_map/pallas_call | solution.py:177
  185.2 23.9 %shard_map.120 = (bf16[1024,256]{1,0:T(8,128)(2,1)}, bf16[1024,512]{1,0:T(8,128)(2,1)}, bf16[5,256,256]{2,1,0:T(8,128)(2,1)}) custom-call(bf16[1024,8192]{1,0:T(8,128)(2,1)} %get-tuple-element.10.sig_ref, bf16[8192,768]{1,0:T(8,128)(2,1)} %get-tuple-element.11.low_ref, bf16[1024,768]{1,0:T(8,128)(2,1)} %get-tuple-element.21.low_ref.own_ref, ...), custom_call_target="tpu_custom_call" | custom-call | tf_op jit(solution)/shard_map/pallas_call | solution.py:244
  209.1 0.0 copy-start.7
  209.1 0.0 copy-start.1
  209.1 36.5 %shard_map.121 = bf16[1280,256]{1,0:T(8,128)(2,1)} custom-call(bf16[1280,256]{1,0:T(8,128)(2,1)} %bitcast.30), custom_call_target="tpu_custom_call" | custom-call | tf_op jit(solution)/shard_map/pallas_call | solution.py:311
  245.6 1.2 convert_element_type.23
  246.9 0.0 copy-start.6
  246.9 0.0 copy-start.3
  246.9 0.0 copy-done
  247.0 0.1 fusion.5
  247.0 0.4 fusion.1
  247.4 0.0 copy-start.2
  247.5 0.2 copy.15
  247.7 0.4 copy-done.6
  248.0 0.2 copy.14
  248.2 0.6 fusion
  248.9 1.0 copy.17
  (14 shorter events, 0.1 us)
Async XLA Ops:
  0.6 1.8 copy-start.8
  0.6 2.1 copy-start.4
  0.7 2.1 copy-start.5
  209.1 37.8 %copy-start.7 = (f32[1,256,256]{2,1,0:T(8,128)S(1)}, f32[1,256,256]{2,1,0:T(8,128)}, u32[]{:S(2)}) copy-start(f32[1,256,256]{2,1,0:T(8,128)} %param.12) | copy-start | bytes 786436
  209.1 38.0 %copy-start.1 = (bf16[2,256,256]{2,1,0:T(8,128)(2,1)S(1)}, bf16[2,256,256]{2,1,0:T(8,128)(2,1)}, u32[]{:S(2)}) copy-start(bf16[2,256,256]{2,1,0:T(8,128)(2,1)} %link_ref.1) | copy-start | bytes 786436
  245.6 1.3 copy-start
  246.9 1.1 copy-start.6
  246.9 1.9 copy-start.3
  247.4 2.4 copy-start.2

commit v3 on v2

--- a/solution.py
+++ b/solution.py
@@ -8,7 +8,7 @@
 from jax.sharding import PartitionSpec as P
 
 KIDS = 2
-PIECES = 8
+PIECES = 16
 MESH = pl.DeviceIdType.MESH
 
 

time: 250 us -> 253 us (1.012)
  Pallas kernels: 241 us -> 244 us
    pallas_call x1, Pallas kernels: 180 us -> 183 us  [gather_all(): pl.pallas_call(functools.partial(gather_kernel, line, chips), out_shape=(...]
where the time goes in v3:
time: 253 us
  Pallas kernels  244 us (96%)
  other arithmetic  4.2 us (2%)
  local copies, waits for them, and re-layouts  3.1 us (1%)
    pallas_call x1, Pallas kernels, gather_all(): pl.pallas_call(functools.partial(gather_kernel, line, chips), out_shape=(...  183 us
    pallas_call x1, Pallas kernels, sum_parts(): pl.pallas_call(functools.partial(sum_kernel, count), out_shape=jax.ShapeD...  36.5 us
    pallas_call x1, Pallas kernels, sweep(): pl.pallas_call(functools.partial(sweep_kernel, par_here), grid=(height //...  23.9 us

profile of v3, /device:TPU:20, one launch (start us, length us, event | category | flops | bytes accessed | tf_op | source)
XLA Modules:
  0.0 252.8 jit_solution(4969867379056794026)
XLA Ops:
  0.7 0.8 fusion.4
  1.5 0.1 copy.13
  1.6 0.6 broadcast_in_dim.21
  2.2 0.2 copy.20
  2.5 0.1 broadcast_bitcast_fusion
  2.5 0.2 broadcast_in_dim.20
  2.8 2.1 pad_maximum_fusion
  4.9 183.3 %shard_map.119 = (bf16[1024,8192]{1,0:T(8,128)(2,1)}, bf16[8192,768]{1,0:T(8,128)(2,1)}) custom-call(bf16[1024,2048]{1,0:T(8,128)(2,1)} %tile_ref.1, bf16[1024,768]{1,0:T(8,128)(2,1)} %get-tuple-element.21.low_ref.own_ref), custom_call_target="tpu_custom_call" | custom-call | tf_op jit(solution)/shard_map/pallas_call | solution.py:177
  188.1 23.9 %shard_map.120 = (bf16[1024,256]{1,0:T(8,128)(2,1)}, bf16[1024,512]{1,0:T(8,128)(2,1)}, bf16[5,256,256]{2,1,0:T(8,128)(2,1)}) custom-call(bf16[1024,8192]{1,0:T(8,128)(2,1)} %get-tuple-element.10.sig_ref, bf16[8192,768]{1,0:T(8,128)(2,1)} %get-tuple-element.11.low_ref, bf16[1024,768]{1,0:T(8,128)(2,1)} %get-tuple-element.21.low_ref.own_ref, ...), custom_call_target="tpu_custom_call" | custom-call | tf_op jit(solution)/shard_map/pallas_call | solution.py:244
  212.0 0.0 copy-start.7
  212.0 0.0 copy-start.1
  212.0 36.5 %shard_map.121 = bf16[1280,256]{1,0:T(8,128)(2,1)} custom-call(bf16[1280,256]{1,0:T(8,128)(2,1)} %bitcast.30), custom_call_target="tpu_custom_call" | custom-call | tf_op jit(solution)/shard_map/pallas_call | solution.py:311
  248.6 0.0 copy-start
  248.6 1.2 convert_element_type.23
  249.8 0.0 copy-start.6
  249.9 0.0 copy-start.3
  249.9 0.1 fusion.5
  250.0 0.4 fusion.1
  250.4 0.0 copy-start.2
  250.4 0.2 copy.15
  250.6 0.4 copy-done.6
  251.0 0.2 copy.14
  251.2 0.6 fusion
  251.8 1.0 copy.17
  (14 shorter events, 0.1 us)
Async XLA Ops:
  0.6 1.8 copy-start.8
  0.6 2.1 copy-start.4
  0.7 2.1 copy-start.5
  212.0 37.8 %copy-start.7 = (f32[1,256,256]{2,1,0:T(8,128)S(1)}, f32[1,256,256]{2,1,0:T(8,128)}, u32[]{:S(2)}) copy-start(f32[1,256,256]{2,1,0:T(8,128)} %param.12) | copy-start | bytes 786436
  212.0 38.0 %copy-start.1 = (bf16[2,256,256]{2,1,0:T(8,128)(2,1)S(1)}, bf16[2,256,256]{2,1,0:T(8,128)(2,1)}, u32[]{:S(2)}) copy-start(bf16[2,256,256]{2,1,0:T(8,128)(2,1)} %link_ref.1) | copy-start | bytes 786436
  248.6 1.3 copy-start
  249.8 1.1 copy-start.6
  249.9 1.9 copy-start.3
  250.4 2.4 copy-start.2
